TPU v7x, 32 devices: a whole 2x2x4 slice. The times are simulated.
32 devices in a mesh: member: 2 (over x), pts: 4 (over y, core), sub: 4 (over z).
Axes of the slice: x: 2, y: 2, z: 4, core: 2. Of those that a mesh axis runs over, the one named last changes fastest.
Arguments:
- spectra: float32 [2592, 4, 512], P('member', 'sub', 'pts'), parts along dimension 0, may hold values from 0.2 to 2
- sea_mask: int32 [4, 512], P('sub', 'pts'), may hold values 0 or 1
- wind_speed: float32 [8, 512], P(('member', 'sub'), 'pts'), parts along dimension 0, may hold values from 0.5 to 2
- growth: float32 [1296], replicated, may hold values from 0.02 to 0.2
- damping: float32 [1296], replicated, may hold values from 0.02 to 0.2
- quartets: int32 [1296, 4], replicated, may hold values from 0 to 1295
- coupling: float32 [1296], replicated, may hold values from 0.05 to 0.3
- upwind: int32 [2, 36, 4, 512], P(None, None, 'sub'), may hold values from 0 to 2
- courant: float32 [2, 1296], replicated, may hold values from 0.1 to 0.9
- obs_point: int32 [4096], replicated, may hold values from 0 to 2047
- obs_hs: float32 [4096], replicated, may hold values from 90 to 170
- nearest: int32 [4, 512], P('sub', 'pts'), may hold values from 0 to 4095
Outputs:
- analysis: float32 [2592, 4, 512], P('member', 'sub', 'pts'), parts along dimension 0
- track_heights: float32 [8192], P('member'), parts along dimension 0
There are 2 independent parts, one for each index of `member`. A program takes and returns all parts, laid end to end along the dimension named above; an argument that names none is the same for every part. Nothing has to cross between parts.
All inputs are finite; a program needn't handle non-finite values. No bound on the sum of `sea_mask` on one device may be relied on, other than what follows from the above.
Results may differ from a plain program's by a relative error of at most 0.0001.
Values sent between devices are 32-bit elements; how exact they have to be, the bound alone decides.
A program may use at most 64 MiB of HBM per device.

v0:
```python
import jax
import jax.numpy as jnp
from jax import lax
from jax.sharding import PartitionSpec as P

ND = 36
STEPS = 2


obs_gain = 0.6


def extended(value, sides, width):
    for axis, dim in sides:
        peers, length = (lax.axis_size(axis), value.shape[dim])
        up = [(i, (i + 1) % peers) for i in range(peers - 1)]
        down = [(j, i) for i, j in up]
        last = lax.slice_in_dim(value, length - width, length, axis=dim)
        initial = lax.slice_in_dim(value, 0, width, axis=dim)
        before = lax.ppermute(last, axis, up)
        after = lax.ppermute(initial, axis, down)
        value = jnp.concatenate([before, value, after], axis=dim)
    return value


def block_count(quad_total):
    pieces = 1
    while quad_total // pieces > 256 or quad_total % pieces != 0:
        pieces = pieces + 1
    return pieces


def interact(masked, quartets, coupling):
    bin_total = masked.shape[0]
    quad_total = quartets.shape[0]
    flat_values = masked.reshape(bin_total, -1)
    pieces = block_count(quad_total)
    width = quad_total // pieces
    bin_ids = jnp.arange(bin_total, dtype=jnp.int32)

    def one_block(step, total):
        quads = lax.dynamic_slice_in_dim(quartets, step * width, width, 0)
        weights = lax.dynamic_slice_in_dim(coupling, step * width, width, 0)
        picks = (quads.T[:, :, None] == bin_ids[None, None, :]).astype(jnp.float32)
        values = jnp.einsum("kqb,bp->kqp", picks, flat_values, precision=lax.Precision.HIGHEST)
        first, second, third, fourth = (values[0], values[1], values[2], values[3])
        flux_term = weights[:, None] * (
            first * second * (third + fourth) - third * fourth * (first + second)
        )
        signs = picks[2] + picks[3] - picks[0] - picks[1]
        return total + jnp.einsum("qb,qp->bp", signs, flux_term, precision=lax.Precision.HIGHEST)

    nonlinear = lax.fori_loop(0, pieces, one_block, jnp.zeros_like(flat_values))
    return nonlinear.reshape(masked.shape)


def source_terms(spectrum, sea_mask, wind_speed, growth, damping, quartets, coupling):
    masked = spectrum * sea_mask.astype(jnp.float32)[None]
    mean_energy = jnp.sum(masked, axis=0) / masked.shape[0]
    growth_rate = (
        growth[:, None, None] * wind_speed[None] - damping[:, None, None] * mean_energy[None]
    )
    grown_spec = masked * jnp.exp(growth_rate)
    nonlinear = interact(masked, quartets, coupling)
    return jnp.maximum(grown_spec + nonlinear, 0.1 * grown_spec)


def owned_bins(bin_layout):
    width = bin_layout.shape[0]
    first_bin = lax.axis_index("pts") * width
    directions = (first_bin + jnp.arange(width, dtype=jnp.int32)) % ND
    return (first_bin, directions)


def advect_lon(bin_layout, upwind, courant):
    width = bin_layout.shape[0]
    first_bin, directions = owned_bins(bin_layout)
    lon_code = jnp.take(upwind[0], directions, axis=0)
    courant_lon = lax.dynamic_slice_in_dim(courant[0], first_bin, width, 0)[:, None, None]
    from_west = jnp.roll(bin_layout, 1, axis=2)
    from_east = jnp.roll(bin_layout, -1, axis=2)
    upstream = jnp.where(lon_code == 0, from_west, jnp.where(lon_code == 2, from_east, bin_layout))
    return bin_layout - courant_lon * (bin_layout - upstream)


def advect_lat_bins(bin_layout, upwind, courant):
    width = bin_layout.shape[0]
    first_bin, directions = owned_bins(bin_layout)
    lat_code = jnp.take(upwind[1], directions, axis=0)
    courant_lat = lax.dynamic_slice_in_dim(courant[1], first_bin, width, 0)[:, None, None]
    padded = extended(bin_layout, (("sub", 1),), 1)
    upstream = jnp.where(
        lat_code == 0, padded[:, :-2], jnp.where(lat_code == 2, padded[:, 2:], bin_layout)
    )
    return bin_layout - courant_lat * (bin_layout - upstream)


def body(
    spectra,
    sea_mask,
    wind_speed,
    growth,
    damping,
    quartets,
    coupling,
    upwind,
    courant,
    obs_point,
    obs_hs,
    nearest,
):
    spectrum = spectra
    for iteration in range(STEPS):
        spectrum = source_terms(spectrum, sea_mask, wind_speed, growth, damping, quartets, coupling)
        bin_layout = lax.all_to_all(spectrum, "pts", split_axis=0, concat_axis=2, tiled=True)
        bin_layout = advect_lon(bin_layout, upwind, courant)
        bin_layout = advect_lat_bins(bin_layout, upwind, courant)
        spectrum = lax.all_to_all(bin_layout, "pts", split_axis=2, concat_axis=0, tiled=True)
    masked = spectrum * sea_mask.astype(jnp.float32)[None]
    energy = jnp.sum(masked, axis=0)
    wave_height = 4.0 * jnp.sqrt(energy)
    height_field = lax.all_gather(wave_height, "sub", axis=0, tiled=True)
    height_field = lax.all_gather(height_field, "pts", axis=1, tiled=True)
    track_heights = jnp.take(height_field.reshape(-1), obs_point)
    innovation = obs_hs - track_heights
    target = wave_height + obs_gain * jnp.take(innovation, nearest)
    scale_ratio = (jnp.maximum(target, 0.5 * wave_height) / (wave_height + 1e-06)) ** 2
    return (masked * scale_ratio[None], track_heights)


def solution(mesh):
    in_specs = (
        P("member", "sub", "pts"),
        P("sub", "pts"),
        P(("member", "sub"), "pts"),
        P(),
        P(),
        P(),
        P(),
        P(None, None, "sub", None),
        P(),
        P(),
        P(),
        P("sub", "pts"),
    )
    out_specs = (P("member", "sub", "pts"), P("member"))
    return jax.shard_map(body, mesh=mesh, in_specs=in_specs, out_specs=out_specs, check_vma=False)
```

profile of v0, /device:TPU:0, one launch (start us, length us, event | category | flops | bytes accessed | tf_op | source)
XLA Modules:
  0.0 311.4 jit_solution(6424555580533212041)
XLA Ops:
  2.6 68.8 %while.28 = (s32[]{:T(128)}, f32[1296,128]{1,0:T(8,128)S(1)}, s32[1296,4]{0,1:T(4,128)}, f32[1296]{0:T(1024)}, f32[1296,128]{1,0:T(8,128)S(1)}, /*index=5*/s32[]{:T(128)}, s32[]{:T(128)}, s32[]{:T(128)}, s32[]{:T(128)}) while((s32[]{:T(128)}, f32[1296,128]{1,0:T(8,128)S(1)}, s32[1296,4]{0,1:T(4,128)}, f32[1296]{0:T(1024)}, ...), condition=%wide.region_2.0_spmd.clone, body=%wide.region_1.0_spmd.clone.sunk | while | flops 2154660352 | bytes 11849917 | solution.py:53
  9.1 5.0 %convolution_add_fusion.4 = f32[1296,128]{1,0:T(8,128)S(1)} fusion(f32[4,216,1296]{2,1,0:T(8,128)} %fusion.93, f32[1296,128]{1,0:T(8,128)S(1)} %get-tuple-element.383, pred[]{:T(512)S(6)} %compare.6, f32[4,216,128]{2,1,0:T(8,128)S(1)} %fusion.94, f32[216]{0:T(256)S(1)} %dynamic_slice.51), kind=kOutput, calls=%fused_computation.9.clone.1 | convolution fusion | flops 431374464 | bytes 6249313 | tf_op jit(solution)/shard_map/while/body/eval_jaxpr/qb,qp->bp/dot_general | solution.py:51
  20.5 5.0 %convolution_add_fusion.4 = f32[1296,128]{1,0:T(8,128)S(1)} fusion(f32[4,216,1296]{2,1,0:T(8,128)} %fusion.93, f32[1296,128]{1,0:T(8,128)S(1)} %get-tuple-element.383, pred[]{:T(512)S(6)} %compare.6, f32[4,216,128]{2,1,0:T(8,128)S(1)} %fusion.94, f32[216]{0:T(256)S(1)} %dynamic_slice.51), kind=kOutput, calls=%fused_computation.9.clone.1 | convolution fusion | flops 431374464 | bytes 6249313 | tf_op jit(solution)/shard_map/while/body/eval_jaxpr/qb,qp->bp/dot_general | solution.py:51
  32.0 5.0 %convolution_add_fusion.4 = f32[1296,128]{1,0:T(8,128)S(1)} fusion(f32[4,216,1296]{2,1,0:T(8,128)} %fusion.93, f32[1296,128]{1,0:T(8,128)S(1)} %get-tuple-element.383, pred[]{:T(512)S(6)} %compare.6, f32[4,216,128]{2,1,0:T(8,128)S(1)} %fusion.94, f32[216]{0:T(256)S(1)} %dynamic_slice.51), kind=kOutput, calls=%fused_computation.9.clone.1 | convolution fusion | flops 431374464 | bytes 6249313 | tf_op jit(solution)/shard_map/while/body/eval_jaxpr/qb,qp->bp/dot_general | solution.py:51
  43.4 5.0 %convolution_add_fusion.4 = f32[1296,128]{1,0:T(8,128)S(1)} fusion(f32[4,216,1296]{2,1,0:T(8,128)} %fusion.93, f32[1296,128]{1,0:T(8,128)S(1)} %get-tuple-element.383, pred[]{:T(512)S(6)} %compare.6, f32[4,216,128]{2,1,0:T(8,128)S(1)} %fusion.94, f32[216]{0:T(256)S(1)} %dynamic_slice.51), kind=kOutput, calls=%fused_computation.9.clone.1 | convolution fusion | flops 431374464 | bytes 6249313 | tf_op jit(solution)/shard_map/while/body/eval_jaxpr/qb,qp->bp/dot_general | solution.py:51
  54.9 5.0 %convolution_add_fusion.4 = f32[1296,128]{1,0:T(8,128)S(1)} fusion(f32[4,216,1296]{2,1,0:T(8,128)} %fusion.93, f32[1296,128]{1,0:T(8,128)S(1)} %get-tuple-element.383, pred[]{:T(512)S(6)} %compare.6, f32[4,216,128]{2,1,0:T(8,128)S(1)} %fusion.94, f32[216]{0:T(256)S(1)} %dynamic_slice.51), kind=kOutput, calls=%fused_computation.9.clone.1 | convolution fusion | flops 431374464 | bytes 6249313 | tf_op jit(solution)/shard_map/while/body/eval_jaxpr/qb,qp->bp/dot_general | solution.py:51
  66.3 5.0 %convolution_add_fusion.4 = f32[1296,128]{1,0:T(8,128)S(1)} fusion(f32[4,216,1296]{2,1,0:T(8,128)} %fusion.93, f32[1296,128]{1,0:T(8,128)S(1)} %get-tuple-element.383, pred[]{:T(512)S(6)} %compare.6, f32[4,216,128]{2,1,0:T(8,128)S(1)} %fusion.94, f32[216]{0:T(256)S(1)} %dynamic_slice.51), kind=kOutput, calls=%fused_computation.9.clone.1 | convolution fusion | flops 431374464 | bytes 6249313 | tf_op jit(solution)/shard_map/while/body/eval_jaxpr/qb,qp->bp/dot_general | solution.py:51
  78.8 8.5 %all-to-all-done = f32[1296,1,128]{2,1,0:T(1,128)S(1)} async-done(((f32[1296,1,128]{2,1,0:T(1,128)}), f32[1296,1,128]{2,1,0:T(1,128)S(1)}, u32[]{:S(2)}, u32[]{:S(2)}) %all-to-all-start) | async-done | bytes 663584 | tf_op jit(solution)/shard_map/all_to_all | solution.py:115
  87.8 5.5 %reduce.15 = f32[1296,128]{1,0:T(8,128)S(1)} reduce(f32[1296,1,128]{2,1,0:T(1,128)S(1)} %all-to-all-done, f32[]{:T(128)} %broadcast.301), dimensions={1}, to_apply=%all_to_all.52.reduce_sub_computation.3 | reduce | bytes 1327108 | tf_op jit(solution)/shard_map/all_to_all | solution.py:115
  104.4 10.8 %collective-permute-done = f32[324,1,512]{2,1,0:T(1,128)S(1)} collective-permute-done((f32[324,1,512]{2,1,0:T(1,128)S(1)}, f32[324,1,512]{2,1,0:T(1,128)S(1)}, u32[]{:S(2)}, u32[]{:S(2)}) %collective-permute-start) | collective-permute-done | bytes 663584 | tf_op jit(solution)/shard_map/ppermute | solution.py:20
  126.6 11.4 %all-to-all-done.1 = f32[324,1,512]{0,1,2:T(1,128)S(1)} async-done(((f32[324,1,512]{0,1,2:T(1,128)}), f32[324,1,512]{0,1,2:T(1,128)S(1)}, u32[]{:S(2)}, u32[]{:S(2)}) %all-to-all-start.1) | async-done | bytes 663584 | tf_op jit(solution)/shard_map/all_to_all | solution.py:118
  139.5 68.7 %while.29 = (s32[]{:T(128)}, f32[1296,128]{1,0:T(8,128)S(1)}, s32[1296,4]{0,1:T(4,128)}, f32[1296]{0:T(1024)}, f32[1296,128]{1,0:T(8,128)S(1)}, /*index=5*/s32[]{:T(128)}, s32[]{:T(128)}, s32[]{:T(128)}, s32[]{:T(128)}) while((s32[]{:T(128)}, f32[1296,128]{1,0:T(8,128)S(1)}, s32[1296,4]{0,1:T(4,128)}, f32[1296]{0:T(1024)}, ...), condition=%wide.region_5.7_spmd.clone, body=%wide.region_4.6_spmd.clone.sunk | while | flops 2154660352 | bytes 11849917 | solution.py:53
  146.0 5.0 %convolution_add_fusion.5 = f32[1296,128]{1,0:T(8,128)S(1)} fusion(f32[4,216,1296]{2,1,0:T(8,128)} %fusion.98, f32[1296,128]{1,0:T(8,128)S(1)} %get-tuple-element.410, pred[]{:T(512)S(6)} %compare.7, f32[4,216,128]{2,1,0:T(8,128)S(1)} %fusion.99, f32[216]{0:T(256)S(1)} %dynamic_slice.53), kind=kOutput, calls=%fused_computation.35.clone.1 | convolution fusion | flops 431374464 | bytes 6249313 | tf_op jit(solution)/shard_map/while/body/eval_jaxpr/qb,qp->bp/dot_general | solution.py:51
  157.4 5.0 %convolution_add_fusion.5 = f32[1296,128]{1,0:T(8,128)S(1)} fusion(f32[4,216,1296]{2,1,0:T(8,128)} %fusion.98, f32[1296,128]{1,0:T(8,128)S(1)} %get-tuple-element.410, pred[]{:T(512)S(6)} %compare.7, f32[4,216,128]{2,1,0:T(8,128)S(1)} %fusion.99, f32[216]{0:T(256)S(1)} %dynamic_slice.53), kind=kOutput, calls=%fused_computation.35.clone.1 | convolution fusion | flops 431374464 | bytes 6249313 | tf_op jit(solution)/shard_map/while/body/eval_jaxpr/qb,qp->bp/dot_general | solution.py:51
  168.9 5.0 %convolution_add_fusion.5 = f32[1296,128]{1,0:T(8,128)S(1)} fusion(f32[4,216,1296]{2,1,0:T(8,128)} %fusion.98, f32[1296,128]{1,0:T(8,128)S(1)} %get-tuple-element.410, pred[]{:T(512)S(6)} %compare.7, f32[4,216,128]{2,1,0:T(8,128)S(1)} %fusion.99, f32[216]{0:T(256)S(1)} %dynamic_slice.53), kind=kOutput, calls=%fused_computation.35.clone.1 | convolution fusion | flops 431374464 | bytes 6249313 | tf_op jit(solution)/shard_map/while/body/eval_jaxpr/qb,qp->bp/dot_general | solution.py:51
  180.3 5.0 %convolution_add_fusion.5 = f32[1296,128]{1,0:T(8,128)S(1)} fusion(f32[4,216,1296]{2,1,0:T(8,128)} %fusion.98, f32[1296,128]{1,0:T(8,128)S(1)} %get-tuple-element.410, pred[]{:T(512)S(6)} %compare.7, f32[4,216,128]{2,1,0:T(8,128)S(1)} %fusion.99, f32[216]{0:T(256)S(1)} %dynamic_slice.53), kind=kOutput, calls=%fused_computation.35.clone.1 | convolution fusion | flops 431374464 | bytes 6249313 | tf_op jit(solution)/shard_map/while/body/eval_jaxpr/qb,qp->bp/dot_general | solution.py:51
  203.2 5.0 %convolution_add_fusion.5 = f32[1296,128]{1,0:T(8,128)S(1)} fusion(f32[4,216,1296]{2,1,0:T(8,128)} %fusion.98, f32[1296,128]{1,0:T(8,128)S(1)} %get-tuple-element.410, pred[]{:T(512)S(6)} %compare.7, f32[4,216,128]{2,1,0:T(8,128)S(1)} %fusion.99, f32[216]{0:T(256)S(1)} %dynamic_slice.53), kind=kOutput, calls=%fused_computation.35.clone.1 | convolution fusion | flops 431374464 | bytes 6249313 | tf_op jit(solution)/shard_map/while/body/eval_jaxpr/qb,qp->bp/dot_general | solution.py:51
  208.7 12.7 %all_to_all.72 = f32[1296,1,128]{2,1,0:T(1,128)S(1)} all-to-all(f32[1296,1,128]{2,1,0:T(1,128)S(1)} %bitcast.142), channel_id=1, replica_groups=mesh['member'=2,'pts'=4,'sub'=4] {'pts'}, dimensions={0} | all-to-all | bytes 1327104 | tf_op jit(solution)/shard_map/all_to_all | solution.py:115
  221.4 5.5 %reduce.16 = f32[1296,128]{1,0:T(8,128)S(1)} reduce(f32[1296,1,128]{2,1,0:T(1,128)S(1)} %all_to_all.72, f32[]{:T(128)} %broadcast.301), dimensions={1}, to_apply=%all_to_all.60.reduce_sub_computation.3 | reduce | bytes 1327108 | tf_op jit(solution)/shard_map/all_to_all | solution.py:115
  235.6 13.0 %collective-permute-done.2 = f32[324,1,512]{2,1,0:T(1,128)S(1)} collective-permute-done((f32[324,1,512]{2,1,0:T(1,128)S(1)}, f32[324,1,512]{2,1,0:T(1,128)S(1)}, u32[]{:S(2)}, u32[]{:S(2)}) %collective-permute-start.2) | collective-permute-done | bytes 663584 | tf_op jit(solution)/shard_map/ppermute | solution.py:20
  258.4 11.6 %all-to-all-done.3 = f32[324,1,512]{0,1,2:T(1,128)S(1)} async-done(((f32[324,1,512]{0,1,2:T(1,128)}), f32[324,1,512]{0,1,2:T(1,128)S(1)}, u32[]{:S(2)}, u32[]{:S(2)}) %all-to-all-start.3) | async-done | bytes 663584 | tf_op jit(solution)/shard_map/all_to_all | solution.py:118
  271.5 9.0 %all-gather.1 = f32[4,1,128]{2,1,0:T(1,128)S(1)} all-gather(f32[1,1,128]{2,1,0:T(1,128)S(1)} %multiply_bitcast_fusion.2), channel_id=2, replica_groups=mesh['member'=2,'pts'=4,'sub'=4] {'sub'}, dimensions={0}, use_global_device_ids=true | all-gather | bytes 2560 | tf_op jit(solution)/shard_map/all_gather | solution.py:122
  280.5 5.2 %all_gather.7 = f32[4,512]{1,0:T(4,128)S(1)} all-gather(f32[4,128]{1,0:T(4,128)S(1)} %bitcast.145), channel_id=1, replica_groups=mesh['member'=2,'pts'=4,'sub'=4] {'pts'}, dimensions={1}, use_global_device_ids=true | all-gather | bytes 10240 | tf_op jit(solution)/shard_map/all_gather | solution.py:123
  285.7 23.0 %gather_fusion = f32[4096]{0:T(1024)S(1)} fusion(f32[2048]{0:T(1024)S(1)} %bitcast.125, s32[4096]{0:T(1024)S(1)} %fusion.63), kind=kCustom, calls=%fused_computation.2 | custom fusion | bytes 49152 | tf_op jit(solution)/shard_map/jit(_take)/gather | solution.py:124
  (138 shorter events, 138.3 us)
Async XLA Ops:
  2.6 68.8 %copy-start = (f32[1296,1,128]{2,1,0:T(1,128)S(1)}, f32[1296,1,128]{2,1,0:T(1,128)}, u32[]{:S(2)}) copy-start(f32[1296,1,128]{2,1,0:T(1,128)} %param.18) | copy-start | bytes 1990660
  2.6 68.8 %copy-start.3 = (f32[1296]{0:T(1024)S(1)}, f32[1296]{0:T(1024)}, u32[]{:S(2)}) copy-start(f32[1296]{0:T(1024)} %param.22) | copy-start | bytes 15556
  2.6 68.8 %copy-start.4 = (f32[1296]{0:T(1024)S(1)}, f32[1296]{0:T(1024)}, u32[]{:S(2)}) copy-start(f32[1296]{0:T(1024)} %param.21) | copy-start | bytes 15556
  2.6 68.8 %copy-start.7 = (f32[1,128]{1,0:T(1,128)S(1)}, f32[1,128]{1,0:T(1,128)}, u32[]{:S(2)}) copy-start(f32[1,128]{1,0:T(1,128)} %param.20) | copy-start | bytes 1540
  71.4 5.5 %copy-start.1 = (s32[2,36,1,512]{3,2,1,0:T(1,128)S(1)}, s32[2,36,1,512]{3,2,1,0:T(1,128)}, u32[]{:S(2)}) copy-start(s32[2,36,1,512]{3,2,1,0:T(1,128)} %param.25) | copy-start | bytes 442372
  72.7 14.6 %all-to-all-start = ((f32[1296,1,128]{2,1,0:T(1,128)}), f32[1296,1,128]{2,1,0:T(1,128)S(1)}, u32[]{:S(2)}, u32[]{:S(2)}) async-start(f32[1296,1,128]{2,1,0:T(1,128)} %bitcast.5), calls=%async_computation | async-start | bytes 1327104 | tf_op jit(solution)/shard_map/all_to_all | solution.py:115
  77.0 1.7 copy-start.6
  97.2 18.1 %collective-permute-start = (f32[324,1,512]{2,1,0:T(1,128)S(1)}, f32[324,1,512]{2,1,0:T(1,128)S(1)}, u32[]{:S(2)}, u32[]{:S(2)}) collective-permute-start(f32[324,1,512]{2,1,0:T(1,128)S(1)} %copy.95), channel_id=1, source_target_pairs={{0,1},{1,2},{2,3},{4,5},{5,6},{6,7},{8,9},{9,10},{10,11},{12,13},{... | collective-permute-start | bytes 1990664 | tf_op jit(solution)/shard_map/ppermute | solution.py:20
  101.4 18.2 %collective-permute-start.1 = (f32[324,1,512]{2,1,0:T(1,128)S(1)}, f32[324,1,512]{2,1,0:T(1,128)}, u32[]{:S(2)}, u32[]{:S(2)}) collective-permute-start(f32[324,1,512]{2,1,0:T(1,128)S(1)} %copy.95), channel_id=1, source_target_pairs={{1,0},{2,1},{3,2},{5,4},{6,5},{7,6},{9,8},{10,9},{11,10},{13,12},{... | collective-permute-start | bytes 1990664 | tf_op jit(solution)/shard_map/ppermute | solution.py:21
  122.9 15.1 %all-to-all-start.1 = ((f32[324,1,512]{0,1,2:T(1,128)}), f32[324,1,512]{0,1,2:T(1,128)S(1)}, u32[]{:S(2)}, u32[]{:S(2)}) async-start(f32[324,1,512]{0,1,2:T(1,128)} %copy.99), calls=%async_computation.1 | async-start | bytes 1572864 | tf_op jit(solution)/shard_map/all_to_all | solution.py:118
  230.8 17.8 %collective-permute-start.2 = (f32[324,1,512]{2,1,0:T(1,128)S(1)}, f32[324,1,512]{2,1,0:T(1,128)S(1)}, u32[]{:S(2)}, u32[]{:S(2)}) collective-permute-start(f32[324,1,512]{2,1,0:T(1,128)S(1)} %copy.111), channel_id=1, source_target_pairs={{0,1},{1,2},{2,3},{4,5},{5,6},{6,7},{8,9},{9,10},{10,11},{12,13},{... | collective-permute-start | bytes 1990664 | tf_op jit(solution)/shard_map/ppermute | solution.py:20
  234.3 18.5 %collective-permute-start.3 = (f32[324,1,512]{2,1,0:T(1,128)S(1)}, f32[324,1,512]{2,1,0:T(1,128)S(1)}, u32[]{:S(2)}, u32[]{:S(2)}) collective-permute-start(f32[324,1,512]{2,1,0:T(1,128)S(1)} %copy.111), channel_id=1, source_target_pairs={{1,0},{2,1},{3,2},{5,4},{6,5},{7,6},{9,8},{10,9},{11,10},{13,12},{... | collective-permute-start | bytes 1990664 | tf_op jit(solution)/shard_map/ppermute | solution.py:21
  253.0 5.4 %copy-start.8 = (s32[1,128]{1,0:T(1,128)S(1)}, s32[1,128]{1,0:T(1,128)}, u32[]{:S(2)}) copy-start(s32[1,128]{1,0:T(1,128)} %param.29) | copy-start | bytes 1540
  253.0 5.4 %copy-start.2 = (s32[4096]{0:T(1024)S(1)}, s32[4096]{0:T(1024)}, u32[]{:S(2)}) copy-start(s32[4096]{0:T(1024)} %param.27) | copy-start | bytes 49156
  254.9 15.1 %all-to-all-start.3 = ((f32[324,1,512]{0,1,2:T(1,128)}), f32[324,1,512]{0,1,2:T(1,128)S(1)}, u32[]{:S(2)}, u32[]{:S(2)}) async-start(f32[324,1,512]{0,1,2:T(1,128)} %copy.115), calls=%async_computation.3 | async-start | bytes 1572864 | tf_op jit(solution)/shard_map/all_to_all | solution.py:118
  285.7 23.0 %copy-start.5 = (f32[4096]{0:T(1024)S(1)}, f32[4096]{0:T(1024)}, u32[]{:S(2)}) copy-start(f32[4096]{0:T(1024)} %param.28) | copy-start | bytes 49156
where the time goes:
time: 313 us; the launch traced here: 311 us
  matrix products  87.9 us (28%)
  waiting for transfers between devices  63.7 us (20%)
  local copies, waits for them, and re-layouts  59.2 us (19%)
  other arithmetic  50.3 us (16%)
  blocking collectives  26.9 us (9%)
  starting transfers between devices  21.7 us (7%)
    dot_general x12, matrix products, one_block(): jnp.einsum('qb,qp->bp', signs, flux_term, precision=lax.Precision.HIGHEST)  60.3 us
    convert_element_type x12, other arithmetic, one_block(): picks = (quads.T[:, :, None] == bin_ids[None, None, :]).astype(jnp.float32)  30.6 us
    dot_general x12, matrix products, one_block(): jnp.einsum('kqb,bp->kqp', picks, flat_values, precision=lax.Precision.HIG...  27.6 us
    ppermute x2, waiting for transfers between devices, extended(): before = lax.ppermute(last, axis, up)  23.9 us
    gather x1, local copies, waits for them, and re-layouts, body(): track_heights = jnp.take(height_field.reshape(-1), obs_point)  23 us
    all_to_all x2, waiting for transfers between devices, body(): lax.all_to_all(bin_layout, 'pts', split_axis=2, concat_axis=0, tiled=True)  23 us
    all_to_all x1, blocking collectives, body(): lax.all_to_all(spectrum, 'pts', split_axis=0, concat_axis=2, tiled=True)  12.7 us
    all_to_all x2, other arithmetic, body(): lax.all_to_all(spectrum, 'pts', split_axis=0, concat_axis=2, tiled=True)  11 us
  transfers between devices with their start and end apart: 7, of which 7 were waited for; matrix products, arithmetic and copies ran while one was open for 1% of the time, Pallas kernels for 0%

commit v1 on v0

v1 whole, which is shorter than its diff:
```python
import functools

import jax
import jax.numpy as jnp
from jax import lax
from jax.experimental import pallas as pl
from jax.experimental.pallas import tpu as pltpu
from jax.sharding import PartitionSpec as P

ND = 36
STEPS = 2
LANES = 128
TILE = 2 * ND
OBS_GAIN = 0.6
MESH = pl.DeviceIdType.MESH
EXACT = lax.Precision.HIGHEST


def row_chunks(total, width):
    starts = list(range(0, total - width + 1, width))
    ends = starts[1:] + [total]
    return tuple((s, e - s) for s, e in zip(starts, ends))


def block_rows(total, most):
    best = 16
    for rows in range(16, most + 1, 16):
        if total % rows == 0:
            best = rows
    return best


def halves(value):
    high = value.astype(jnp.bfloat16)
    low = (value - high.astype(jnp.float32)).astype(jnp.bfloat16)
    return high, low


def thirds(value):
    first = value.astype(jnp.bfloat16)
    rest = value - first.astype(jnp.float32)
    second, third = halves(rest)
    return first, second, third


def one_hot_rows(index_row, height):
    rows = lax.broadcasted_iota(jnp.int32, (height, index_row.shape[1]), 0)
    return jnp.where(rows == index_row, 1.0, 0.0)


def table_pick(table, picks, row_row):
    first, second, third = thirds(table)
    by_lane = (
        jnp.dot(first, picks, preferred_element_type=jnp.float32)
        + jnp.dot(second, picks, preferred_element_type=jnp.float32)
        + jnp.dot(third, picks, preferred_element_type=jnp.float32)
    )
    chosen = one_hot_rows(row_row, table.shape[0])
    return jnp.sum(by_lane * chosen, axis=0, keepdims=True)


def kernel(
    pts_total,
    sub_total,
    chunks,
    quad_block,
    spec_ref,
    mask_ref,
    wind_ref,
    cols_ref,
    quad_ref,
    quad_t_ref,
    codes_ref,
    obs_row_ref,
    obs_table_ref,
    hs_table_ref,
    near_ref,
    out_ref,
    track_ref,
    picks,
    signs,
    gathered,
    split_values,
    split_flux,
    masked_ref,
    sourced,
    advected,
    lower,
    higher,
    lon_codes,
    lat_codes,
    edge_out,
    edge_in,
    obs_picks,
    heights,
    west_send,
    west_recv,
    east_send,
    east_recv,
    up_send,
    up_recv,
    down_send,
    down_recv,
    height_send,
    height_recv,
):
    member = lax.axis_index("member")
    my_pts = lax.axis_index("pts")
    my_sub = lax.axis_index("sub")
    peers = pts_total * sub_total
    me = my_sub * pts_total + my_pts
    west = (member, lax.rem(my_pts + pts_total - 1, pts_total), my_sub)
    east = (member, lax.rem(my_pts + 1, pts_total), my_sub)
    above = (member, my_pts, my_sub + 1)
    below = (member, my_pts, my_sub - 1)
    has_above = my_sub < sub_total - 1
    has_below = my_sub > 0
    bins = spec_ref.shape[0]
    quads = quad_ref.shape[0]
    quad_blocks = quads // quad_block

    def peer_id(offset):
        peer = lax.rem(me + offset, peers)
        return peer, (member, lax.rem(peer, pts_total), lax.div(peer, pts_total))

    barrier = pltpu.get_barrier_semaphore()

    @pl.loop(1, peers)
    def _(offset):
        pl.semaphore_signal(barrier, inc=1, device_id=peer_id(offset)[1], device_id_type=MESH)

    mask = mask_ref[...].astype(jnp.float32)
    wind = wind_ref[...]

    def take_chunk(value, start, size):
        value = value * mask
        masked_ref[pl.ds(start, size), :] = value
        high, low = halves(value)
        split_values[pl.ds(start, size), :LANES] = high
        split_values[pl.ds(start, size), LANES:] = low
        return jnp.sum(value, axis=0, keepdims=True)

    energy = jnp.zeros((1, LANES), jnp.float32)
    for start, size in chunks:
        energy = energy + take_chunk(spec_ref[pl.ds(start, size), :], start, size)

    part = 48 if quad_block % 48 == 0 else 16

    @pl.loop(0, quad_blocks)
    def _(block):
        for member_of_quad in range(4):
            @pl.loop(0, quad_block // part)
            def _(inner):
                row = pl.multiple_of(block * quad_block + inner * part, part)
                index = quad_ref[pl.ds(row, part), member_of_quad : member_of_quad + 1]
                lanes = lax.broadcasted_iota(jnp.int32, (part, bins), 1)
                hot = jnp.where(lanes == index, 1.0, 0.0).astype(jnp.bfloat16)
                to = pl.multiple_of(
                    block * (4 * quad_block) + member_of_quad * quad_block + inner * part, part
                )
                picks[pl.ds(to, part), :] = hot

    part_b = 48 if bins % 48 == 0 else 16

    @pl.loop(0, bins // part_b)
    def _(block):
        row = pl.multiple_of(block * part_b, part_b)
        rows = lax.broadcasted_iota(jnp.int32, (part_b, quads), 0) + row
        total = jnp.zeros((part_b, quads), jnp.float32)
        for member_of_quad, sign in enumerate((-1.0, -1.0, 1.0, 1.0)):
            index = quad_t_ref[member_of_quad : member_of_quad + 1, :]
            total = total + jnp.where(rows == index, sign, 0.0)
        signs[pl.ds(row, part_b), :] = total.astype(jnp.bfloat16)

    @pl.loop(0, bins // TILE)
    def _(block):
        row = pl.multiple_of(block * TILE, TILE)
        lon_codes[pl.ds(row, TILE), :] = codes_ref[0]
        lat_codes[pl.ds(row, TILE), :] = codes_ref[1]

    @pl.when(jnp.logical_not(has_below))
    def _():
        lower[...] = jnp.zeros_like(lower)

    @pl.when(jnp.logical_not(has_above))
    def _():
        higher[...] = jnp.zeros_like(higher)

    def gather_block(block, start, size):
        rows = pl.ds(pl.multiple_of(block * (4 * quad_block), 4 * quad_block), 4 * quad_block)
        got = jnp.dot(
            picks[rows, pl.ds(start, size)],
            split_values[pl.ds(start, size), :],
            preferred_element_type=jnp.float32,
        )
        return rows, got[:, :LANES] + got[:, LANES:]

    def flux_block(block, got):
        rows = pl.ds(pl.multiple_of(block * quad_block, quad_block), quad_block)
        one, two, three, four = (got[k * quad_block : (k + 1) * quad_block] for k in range(4))
        weight = cols_ref[rows, 4:5]
        flux = weight * (one * two * (three + four) - three * four * (one + two))
        high, low = halves(flux)
        split_flux[rows, :LANES] = high
        split_flux[rows, LANES:] = low

    lane = lax.broadcasted_iota(jnp.int32, (1, LANES), 1)
    sel_row = lax.broadcasted_iota(jnp.int32, (8, LANES), 0)
    sel_lane = lax.broadcasted_iota(jnp.int32, (8, LANES), 1)
    edge_select = jnp.where(
        ((sel_row == 0) & (sel_lane == 0)) | ((sel_row == 1) & (sel_lane == LANES - 1)), 1.0, 0.0
    )
    put_row = lax.broadcasted_iota(jnp.int32, (16, LANES), 0)
    put_lane = lax.broadcasted_iota(jnp.int32, (16, LANES), 1)
    edge_place = jnp.where(
        ((put_row == 1) & (put_lane == 0)) | ((put_row == 8) & (put_lane == LANES - 1)), 1.0, 0.0
    )

    def edge_copies(step, c):
        to_west = pltpu.make_async_remote_copy(
            src_ref=edge_out.at[step, c],
            dst_ref=edge_in.at[step, c, 1],
            send_sem=west_send.at[step, c],
            recv_sem=west_recv.at[step, c],
            device_id=west,
            device_id_type=MESH,
        )
        to_east = pltpu.make_async_remote_copy(
            src_ref=edge_out.at[step, c],
            dst_ref=edge_in.at[step, c, 0],
            send_sem=east_send.at[step, c],
            recv_sem=east_recv.at[step, c],
            device_id=east,
            device_id_type=MESH,
        )
        return to_west, to_east

    def row_copies(step, c):
        start, size = chunks[c]
        rows = pl.ds(start, size)
        to_above = pltpu.make_async_remote_copy(
            src_ref=advected.at[step, rows],
            dst_ref=lower.at[step, rows],
            send_sem=up_send.at[step, c],
            recv_sem=up_recv.at[step, c],
            device_id=above,
            device_id_type=MESH,
        )
        to_below = pltpu.make_async_remote_copy(
            src_ref=advected.at[step, rows],
            dst_ref=higher.at[step, rows],
            send_sem=down_send.at[step, c],
            recv_sem=down_recv.at[step, c],
            device_id=below,
            device_id_type=MESH,
        )
        return to_above, to_below

    def source_chunk(step, c, mean):
        start, size = chunks[c]
        rows = pl.ds(start, size)
        change = jnp.dot(signs[rows, :], split_flux[...], preferred_element_type=jnp.float32)
        change = change[:, :LANES] + change[:, LANES:]
        rate = cols_ref[rows, 0:1] * wind - cols_ref[rows, 1:2] * mean
        grown = masked_ref[rows, :] * jnp.exp(rate)
        value = jnp.maximum(grown + change, 0.1 * grown)
        sourced[rows, :] = value
        edge_out[step, c, :, :size] = lax.dot_general(
            edge_select,
            value,
            (((1,), (1,)), ((), ())),
            precision=EXACT,
            preferred_element_type=jnp.float32,
        )
        for copy in edge_copies(step, c):
            copy.start()

    def lon_chunk(step, c):
        start, size = chunks[c]
        rows = pl.ds(start, size)
        to_west, to_east = edge_copies(step, c)
        to_west.wait_recv()
        to_east.wait_recv()
        edges = jnp.concatenate([edge_in[step, c, 0, :, :size], edge_in[step, c, 1, :, :size]], axis=0)
        outside = lax.dot_general(
            edges,
            edge_place,
            (((0,), (0,)), ((), ())),
            precision=EXACT,
            preferred_element_type=jnp.float32,
        )
        value = sourced[rows, :]
        from_west = jnp.where(lane == 0, outside, pltpu.roll(value, 1, 1))
        from_east = jnp.where(lane == LANES - 1, outside, pltpu.roll(value, LANES - 1, 1))
        code = lon_codes[rows, :]
        upstream = jnp.where(code == 0, from_west, jnp.where(code == 2, from_east, value))
        advected[step, rows, :] = value - cols_ref[rows, 2:3] * (value - upstream)
        to_above, to_below = row_copies(step, c)

        @pl.when(has_above)
        def _():
            to_above.start()

        @pl.when(has_below)
        def _():
            to_below.start()

    def lat_chunk(step, c):
        start, size = chunks[c]
        rows = pl.ds(start, size)
        to_above, to_below = row_copies(step, c)

        @pl.when(has_below)
        def _():
            to_above.wait_recv()

        @pl.when(has_above)
        def _():
            to_below.wait_recv()

        value = advected[step, rows, :]
        code = lat_codes[rows, :]
        upstream = jnp.where(
            code == 0, lower[step, rows, :], jnp.where(code == 2, higher[step, rows, :], value)
        )
        return value - cols_ref[rows, 3:4] * (value - upstream)

    def source_and_lon(step, mean):
        for c in range(len(chunks)):
            source_chunk(step, c, mean)
            if c > 0:
                lon_chunk(step, c - 1)
        lon_chunk(step, len(chunks) - 1)

    @pl.loop(0, quad_blocks)
    def _(block):
        flux_block(block, gather_block(block, 0, bins)[1])

    pl.semaphore_wait(barrier, peers - 1)
    source_and_lon(0, energy / bins)

    obs_point = obs_row_ref[...]
    obs_picks[...] = one_hot_rows(lax.rem(obs_point, LANES), LANES).astype(jnp.bfloat16)
    near = near_ref[...]
    near_picks = one_hot_rows(lax.rem(near, LANES), LANES).astype(jnp.bfloat16)
    near_row = lax.div(near, LANES)
    near_hs = table_pick(hs_table_ref[...], near_picks, near_row)
    near_point = table_pick(obs_table_ref[...].astype(jnp.float32), near_picks, near_row)

    for step in range(1, STEPS):
        energy = jnp.zeros((1, LANES), jnp.float32)
        for c, (start, size) in enumerate(chunks):
            energy = energy + take_chunk(lat_chunk(step - 1, c), start, size)

            @pl.loop(0, quad_blocks)
            def _(block):
                rows, got = gather_block(block, start, size)
                if c > 0:
                    got = gathered[rows, :] + got
                if c < len(chunks) - 1:
                    gathered[rows, :] = got
                else:
                    flux_block(block, got)

        source_and_lon(step, energy / bins)

    energy = jnp.zeros((1, LANES), jnp.float32)
    for c, (start, size) in enumerate(chunks):
        value = lat_chunk(STEPS - 1, c) * mask
        masked_ref[pl.ds(start, size), :] = value
        energy = energy + jnp.sum(value, axis=0, keepdims=True)
    wave_height = 4.0 * jnp.sqrt(energy)
    heights[me] = jnp.broadcast_to(wave_height, (8, LANES))

    def height_copy(slot, to):
        return pltpu.make_async_remote_copy(
            src_ref=heights.at[me],
            dst_ref=heights.at[me],
            send_sem=height_send.at[slot],
            recv_sem=height_recv.at[me],
            device_id=to,
            device_id_type=MESH,
        )

    @pl.loop(1, peers)
    def _(offset):
        height_copy(offset, peer_id(offset)[1]).start()

    @pl.loop(1, peers)
    def _(offset):
        peer, to = peer_id(offset)
        pltpu.make_async_remote_copy(
            src_ref=heights.at[me],
            dst_ref=heights.at[peer],
            send_sem=height_send.at[offset],
            recv_sem=height_recv.at[peer],
            device_id=to,
            device_id_type=MESH,
        ).wait_recv()

    table = heights[:, 0, :]
    track = table_pick(table, obs_picks[...], lax.div(obs_point, LANES))
    track_ref[...] = track
    near_point = near_point.astype(jnp.int32)
    near_lane = one_hot_rows(lax.rem(near_point, LANES), LANES).astype(jnp.bfloat16)
    near_track = table_pick(table, near_lane, lax.div(near_point, LANES))
    target = wave_height + OBS_GAIN * (near_hs - near_track)
    ratio = jnp.maximum(target, 0.5 * wave_height) / (wave_height + 1e-6)
    scale = ratio * ratio
    for start, size in chunks:
        out_ref[pl.ds(start, size), :] = masked_ref[pl.ds(start, size), :] * scale

    for step in range(STEPS):
        for c in range(len(chunks)):
            for copy in edge_copies(step, c):
                copy.wait_send()
            to_above, to_below = row_copies(step, c)

            @pl.when(has_above)
            def _():
                to_above.wait_send()

            @pl.when(has_below)
            def _():
                to_below.wait_send()

    @pl.loop(1, peers)
    def _(offset):
        height_copy(offset, peer_id(offset)[1]).wait_send()


def body(
    pts_total,
    sub_total,
    spectra,
    sea_mask,
    wind_speed,
    growth,
    damping,
    quartets,
    coupling,
    upwind,
    courant,
    obs_point,
    obs_hs,
    nearest,
):
    bins = spectra.shape[0]
    quads = quartets.shape[0]
    observations = obs_point.shape[0]
    chunks = row_chunks(bins, 256)
    most = max(size for _, size in chunks)
    wide = -(-most // LANES) * LANES
    quad_block = block_rows(quads, 432)
    peers = pts_total * sub_total
    cols = jnp.stack([growth, damping, courant[0], courant[1], coupling], axis=1)
    codes = lax.dynamic_slice_in_dim(upwind, lax.axis_index("pts") * LANES, LANES, 3)[:, :, 0]
    codes = jnp.concatenate([codes, codes], axis=1)
    f32, bf16 = jnp.float32, jnp.bfloat16
    count = len(chunks)
    vmem = pl.BlockSpec(memory_space=pltpu.VMEM)
    analysis, track = pl.pallas_call(
        functools.partial(kernel, pts_total, sub_total, chunks, quad_block),
        out_shape=(
            jax.ShapeDtypeStruct((bins, LANES), f32),
            jax.ShapeDtypeStruct((1, observations), f32),
        ),
        in_specs=[vmem] * 11,
        out_specs=(vmem, vmem),
        scratch_shapes=[
            pltpu.VMEM((4 * quads, bins), bf16),
            pltpu.VMEM((bins, quads), bf16),
            pltpu.VMEM((4 * quads, LANES), f32),
            pltpu.VMEM((bins, 2 * LANES), bf16),
            pltpu.VMEM((quads, 2 * LANES), bf16),
            pltpu.VMEM((bins, LANES), f32),
            pltpu.VMEM((bins, LANES), f32),
            pltpu.VMEM((STEPS, bins, LANES), f32),
            pltpu.VMEM((STEPS, bins, LANES), f32),
            pltpu.VMEM((STEPS, bins, LANES), f32),
            pltpu.VMEM((bins, LANES), jnp.int32),
            pltpu.VMEM((bins, LANES), jnp.int32),
            pltpu.VMEM((STEPS, count, 8, wide), f32),
            pltpu.VMEM((STEPS, count, 2, 8, wide), f32),
            pltpu.VMEM((LANES, observations), bf16),
            pltpu.VMEM((peers, 8, LANES), f32),
        ]
        + [pltpu.SemaphoreType.DMA((STEPS, count))] * 8
        + [pltpu.SemaphoreType.DMA((peers,))] * 2,
        compiler_params=pltpu.CompilerParams(
            collective_id=0, has_side_effects=True, vmem_limit_bytes=56 * 1024 * 1024
        ),
    )(
        spectra.reshape(bins, LANES),
        sea_mask,
        wind_speed,
        cols,
        quartets,
        quartets.T,
        codes,
        obs_point.reshape(1, observations),
        obs_point.reshape(-1, LANES),
        obs_hs.reshape(-1, LANES),
        nearest,
    )
    return analysis.reshape(bins, 1, LANES), track.reshape(observations)


def solution(mesh):
    in_specs = (
        P("member", "sub", "pts"),
        P("sub", "pts"),
        P(("member", "sub"), "pts"),
        P(),
        P(),
        P(),
        P(),
        P(None, None, "sub", None),
        P(),
        P(),
        P(),
        P("sub", "pts"),
    )
    out_specs = (P("member", "sub", "pts"), P("member"))
    return jax.shard_map(
        functools.partial(body, mesh.shape["pts"], mesh.shape["sub"]),
        mesh=mesh,
        in_specs=in_specs,
        out_specs=out_specs,
        check_vma=False,
    )
```

time: 313 us -> 79.4 us (0.25)
  matrix products: 87.9 us -> 0 us
  Pallas kernels: 0 us -> 71.6 us
  waiting for transfers between devices: 63.7 us -> 0 us
  local copies, waits for them, and re-layouts: 59.2 us -> 6.23 us
  other arithmetic: 50.3 us -> 0.64 us
  blocking collectives: 26.9 us -> 0 us
  starting transfers between devices: 21.7 us -> 0 us
    dot_general x24 -> x0, matrix products: 87.9 us -> none  [the longest x12 60.3 us: one_block(): jnp.einsum('qb,qp->bp', signs, flux_term, precision=lax.Precision.HIGHEST)]
    pallas_call x0 -> x1, Pallas kernels: none -> 71.6 us  [body(): pl.pallas_call(functools.partial(kernel, pts_total, sub_total, chunks, qu...]
    ppermute x4 -> x0, waiting for transfers between devices: 32.3 us -> none  [the longest x2 23.9 us: extended(): before = lax.ppermute(last, axis, up)]
    all_to_all x3 -> x0, waiting for transfers between devices: 31.4 us -> none  [the longest x2 23 us: body(): lax.all_to_all(bin_layout, 'pts', split_axis=2, concat_axis=0, tiled=True)]
    convert_element_type x12 -> x0, other arithmetic: 30.6 us -> none  [one_block(): picks = (quads.T[:, :, None] == bin_ids[None, None, :]).astype(jnp.float32)]
    gather x4 -> x0, local copies, waits for them, and re-layouts: 27.5 us -> none  [the longest x1 23 us: body(): track_heights = jnp.take(height_field.reshape(-1), obs_point)]
    all_gather x2 -> x0, blocking collectives: 14.2 us -> none  [the longest x1 9.05 us: body(): height_field = lax.all_gather(wave_height, 'sub', axis=0, tiled=True)]
    all_to_all x1 -> x0, blocking collectives: 12.7 us -> none  [body(): lax.all_to_all(spectrum, 'pts', split_axis=0, concat_axis=2, tiled=True)]
  transfers between devices with their start and end apart: 7 -> 0, of which waited for: 7 -> 0; matrix products, arithmetic and copies ran while one was open for 1% -> 0% of each run, Pallas kernels for 0% -> 0%
where the time goes in v1:
time: 79.4 us; the launch traced here: 79.2 us
  Pallas kernels  71.6 us (90%)
  local copies, waits for them, and re-layouts  6.23 us (8%)
    pallas_call x1, Pallas kernels, body(): pl.pallas_call(functools.partial(kernel, pts_total, sub_total, chunks, qu...  71.6 us
    unnamed x17, local copies, waits for them, and re-layouts  4.98 us

profile of v1, /device:TPU:0, one launch (start us, length us, event | category | flops | bytes accessed | tf_op | source)
XLA Modules:
  0.0 79.2 jit_solution(3815192061984542903)
XLA Ops:
  0.6 0.0 copy-start
  0.7 0.0 copy-start.4
  0.7 0.0 copy-start.5
  0.7 0.7 copy-done.4
  1.4 0.0 copy-start.6
  1.4 0.0 copy-done.5
  1.4 0.0 copy-start.3
  1.4 0.7 copy-done.6
  2.1 0.0 copy-done.3
  2.1 0.1 stack.15
  2.2 0.0 copy-done
  2.3 0.6 pad_add_fusion.codes_ref
  2.9 0.0 copy-start.1
  2.9 1.1 %copy.29.cols_ref = f32[1296,5]{1,0:T(8,128)} copy(f32[1296,5]{0,1:T(8,128)S(1)} %stack.15) | data formatting | bytes 51840 | tf_op jit(solution)/shard_map/stack | solution.py:456
  4.0 0.0 copy-done.1
  4.0 1.1 %copy.30.quad_ref = s32[1296,4]{1,0:T(8,128)} copy(s32[1296,4]{0,1:T(4,128)S(1)} %copy-done.1) | data formatting | bytes 41472 | tf_op args[5]
  5.1 71.6 %shard_map.131 = (f32[1296,128]{1,0:T(8,128)}, f32[1,4096]{1,0:T(1,128)}) custom-call(f32[1296,128]{1,0:T(8,128)} %bitcast.16, s32[1,128]{1,0:T(1,128)} %mask_ref.1, f32[1,128]{1,0:T(1,128)} %wind_ref.1, f32[1296,5]{1,0:T(8,128)} %copy.29.cols_ref, s32[1296,4]{1,0:T(8,128)} %copy.30.quad_ref, s32[4,1296]{1,0:T(4,128)} %bitcast.19, ...), custom_call_target="tpu_custom_call" | custom-call | tf_op jit(solution)/shard_map/pallas_call | solution.py:462
  76.7 0.0 copy-start.2
  76.8 1.8 %copy.36 = f32[1296,1,128]{2,1,0:T(1,128)} copy(f32[1296,1,128]{2,1,0:T(1,128)} %bitcast.17) | data formatting | bytes 1327104
  78.6 0.0 copy-done.2
  78.6 0.6 copy.37
  (7 shorter events, 0.1 us)
Async XLA Ops:
  0.6 1.5 %copy-start = (s32[2,36,1,512]{3,2,1,0:T(1,128)S(1)}, s32[2,36,1,512]{3,2,1,0:T(1,128)}, u32[]{:S(2)}) copy-start(s32[2,36,1,512]{3,2,1,0:T(1,128)} %param.19) | copy-start | bytes 442372
  0.7 0.7 copy-start.4
  0.7 0.7 copy-start.5
  1.4 0.7 copy-start.6
  1.4 0.7 copy-start.3
  2.9 1.1 %copy-start.1 = (s32[1296,4]{0,1:T(4,128)S(1)}, s32[1296,4]{0,1:T(4,128)}, u32[]{:S(2)}) copy-start(s32[1296,4]{0,1:T(4,128)} %param.17) | copy-start | bytes 62212
  76.7 1.9 %copy-start.2 = (f32[1,4096]{1,0:T(1,128)S(1)}, f32[1,4096]{1,0:T(1,128)}, u32[]{:S(2)}) copy-start(f32[1,4096]{1,0:T(1,128)} %get-tuple-element.5) | copy-start | bytes 49156

commit v2 on v1

--- a/solution.py
+++ b/solution.py
@@ -11,9 +11,9 @@
 STEPS = 2
 LANES = 128
 TILE = 2 * ND
+LAG = 2
 OBS_GAIN = 0.6
 MESH = pl.DeviceIdType.MESH
-EXACT = lax.Precision.HIGHEST
 
 
 def row_chunks(total, width):
@@ -67,22 +67,24 @@
     spec_ref,
     mask_ref,
     wind_ref,
-    cols_ref,
-    quad_ref,
+    growth_ref,
+    damping_ref,
+    courant_ref,
+    coupling_ref,
     quad_t_ref,
-    codes_ref,
+    codes_in_ref,
     obs_row_ref,
     obs_table_ref,
     hs_table_ref,
     near_ref,
-    out_ref,
+    masked_ref,
     track_ref,
+    scale_ref,
     picks,
     signs,
     gathered,
     split_values,
     split_flux,
-    masked_ref,
     sourced,
     advected,
     lower,
@@ -93,6 +95,10 @@
     edge_in,
     obs_picks,
     heights,
+    cols_ref,
+    quad_ref,
+    codes_ref,
+    turn,
     west_send,
     west_recv,
     east_send,
@@ -116,7 +122,7 @@
     has_above = my_sub < sub_total - 1
     has_below = my_sub > 0
     bins = spec_ref.shape[0]
-    quads = quad_ref.shape[0]
+    quads = quad_t_ref.shape[1]
     quad_blocks = quads // quad_block
 
     def peer_id(offset):
@@ -128,6 +134,19 @@
     @pl.loop(1, peers)
     def _(offset):
         pl.semaphore_signal(barrier, inc=1, device_id=peer_id(offset)[1], device_id_type=MESH)
+
+    turn[...] = jnp.zeros_like(turn)
+    turn[0:4, :quads] = quad_t_ref[...].astype(jnp.float32)
+    quad_ref[...] = turn[...].T[:quads].astype(jnp.int32)
+    turn[0, :bins] = growth_ref[...]
+    turn[1, :bins] = damping_ref[...]
+    turn[2:4, :bins] = courant_ref[...]
+    turn[4, :quads] = coupling_ref[...]
+    cols_ref[...] = turn[...].T[:bins]
+    for axis in range(2):
+        mine = codes_in_ref[pl.ds(axis * ND * pts_total + my_pts, ND, stride=pts_total), :]
+        codes_ref[axis, :ND] = mine
+        codes_ref[axis, ND:] = mine
 
     mask = mask_ref[...].astype(jnp.float32)
     wind = wind_ref[...]
@@ -144,33 +163,29 @@
     for start, size in chunks:
         energy = energy + take_chunk(spec_ref[pl.ds(start, size), :], start, size)
 
-    part = 48 if quad_block % 48 == 0 else 16
+    one16 = jnp.bfloat16(1)
+    zero16 = jnp.bfloat16(0)
 
     @pl.loop(0, quad_blocks)
     def _(block):
         for member_of_quad in range(4):
-            @pl.loop(0, quad_block // part)
-            def _(inner):
-                row = pl.multiple_of(block * quad_block + inner * part, part)
-                index = quad_ref[pl.ds(row, part), member_of_quad : member_of_quad + 1]
-                lanes = lax.broadcasted_iota(jnp.int32, (part, bins), 1)
-                hot = jnp.where(lanes == index, 1.0, 0.0).astype(jnp.bfloat16)
-                to = pl.multiple_of(
-                    block * (4 * quad_block) + member_of_quad * quad_block + inner * part, part
-                )
-                picks[pl.ds(to, part), :] = hot
-
-    part_b = 48 if bins % 48 == 0 else 16
-
-    @pl.loop(0, bins // part_b)
-    def _(block):
-        row = pl.multiple_of(block * part_b, part_b)
-        rows = lax.broadcasted_iota(jnp.int32, (part_b, quads), 0) + row
-        total = jnp.zeros((part_b, quads), jnp.float32)
-        for member_of_quad, sign in enumerate((-1.0, -1.0, 1.0, 1.0)):
-            index = quad_t_ref[member_of_quad : member_of_quad + 1, :]
-            total = total + jnp.where(rows == index, sign, 0.0)
-        signs[pl.ds(row, part_b), :] = total.astype(jnp.bfloat16)
+            row = pl.multiple_of(block * quad_block, quad_block)
+            index = quad_ref[pl.ds(row, quad_block), member_of_quad : member_of_quad + 1]
+            lanes = lax.broadcasted_iota(jnp.int32, (quad_block, bins), 1).astype(jnp.int16)
+            index = jnp.broadcast_to(index, (quad_block, LANES)).astype(jnp.int16)
+            index = jnp.concatenate([index] * (-(-bins // LANES)), axis=1)[:, :bins]
+            to = pl.multiple_of(block * (4 * quad_block) + member_of_quad * quad_block, quad_block)
+            picks[pl.ds(to, quad_block), :] = jnp.where(lanes == index, one16, zero16)
+
+    def sign_rows(row, size):
+        rows = (lax.broadcasted_iota(jnp.int32, (size, quads), 0) + row).astype(jnp.int16)
+        total = None
+        for member_of_quad, sign in enumerate((-one16, -one16, one16, one16)):
+            index = jnp.broadcast_to(quad_t_ref[member_of_quad : member_of_quad + 1, :], (16, quads))
+            index = jnp.concatenate([index.astype(jnp.int16)] * (size // 16), axis=0)
+            term = jnp.where(rows == index, sign, zero16)
+            total = term if total is None else total + term
+        signs[pl.ds(row, size), :] = total
 
     @pl.loop(0, bins // TILE)
     def _(block):
@@ -205,16 +220,16 @@
         split_flux[rows, LANES:] = low
 
     lane = lax.broadcasted_iota(jnp.int32, (1, LANES), 1)
-    sel_row = lax.broadcasted_iota(jnp.int32, (8, LANES), 0)
-    sel_lane = lax.broadcasted_iota(jnp.int32, (8, LANES), 1)
+    sel_row = lax.broadcasted_iota(jnp.int32, (8, 2 * LANES), 0)
+    sel_lane = lax.rem(lax.broadcasted_iota(jnp.int32, (8, 2 * LANES), 1), LANES)
     edge_select = jnp.where(
         ((sel_row == 0) & (sel_lane == 0)) | ((sel_row == 1) & (sel_lane == LANES - 1)), 1.0, 0.0
-    )
-    put_row = lax.broadcasted_iota(jnp.int32, (16, LANES), 0)
-    put_lane = lax.broadcasted_iota(jnp.int32, (16, LANES), 1)
+    ).astype(jnp.bfloat16)
+    put_row = lax.rem(lax.broadcasted_iota(jnp.int32, (32, LANES), 0), 16)
+    put_lane = lax.broadcasted_iota(jnp.int32, (32, LANES), 1)
     edge_place = jnp.where(
         ((put_row == 1) & (put_lane == 0)) | ((put_row == 8) & (put_lane == LANES - 1)), 1.0, 0.0
-    )
+    ).astype(jnp.bfloat16)
 
     def edge_copies(step, c):
         to_west = pltpu.make_async_remote_copy(
@@ -259,17 +274,15 @@
     def source_chunk(step, c, mean):
         start, size = chunks[c]
         rows = pl.ds(start, size)
-        change = jnp.dot(signs[rows, :], split_flux[...], preferred_element_type=jnp.float32)
-        change = change[:, :LANES] + change[:, LANES:]
+        change = sourced[rows, :]
         rate = cols_ref[rows, 0:1] * wind - cols_ref[rows, 1:2] * mean
         grown = masked_ref[rows, :] * jnp.exp(rate)
         value = jnp.maximum(grown + change, 0.1 * grown)
         sourced[rows, :] = value
         edge_out[step, c, :, :size] = lax.dot_general(
             edge_select,
-            value,
+            jnp.concatenate(halves(value), axis=1),
             (((1,), (1,)), ((), ())),
-            precision=EXACT,
             preferred_element_type=jnp.float32,
         )
         for copy in edge_copies(step, c):
@@ -283,10 +296,9 @@
         to_east.wait_recv()
         edges = jnp.concatenate([edge_in[step, c, 0, :, :size], edge_in[step, c, 1, :, :size]], axis=0)
         outside = lax.dot_general(
-            edges,
+            jnp.concatenate(halves(edges), axis=0),
             edge_place,
             (((0,), (0,)), ((), ())),
-            precision=EXACT,
             preferred_element_type=jnp.float32,
         )
         value = sourced[rows, :]
@@ -326,15 +338,22 @@
         return value - cols_ref[rows, 3:4] * (value - upstream)
 
     def source_and_lon(step, mean):
-        for c in range(len(chunks)):
-            source_chunk(step, c, mean)
-            if c > 0:
-                lon_chunk(step, c - 1)
-        lon_chunk(step, len(chunks) - 1)
+        change = jnp.dot(signs[...], split_flux[...], preferred_element_type=jnp.float32)
+        sourced[...] = change[:, :LANES] + change[:, LANES:]
+        for c in range(len(chunks) + LAG):
+            if c < len(chunks):
+                source_chunk(step, c, mean)
+            if c >= LAG:
+                lon_chunk(step, c - LAG)
+
+    sign_part = block_rows(bins // quad_blocks, 144)
 
     @pl.loop(0, quad_blocks)
     def _(block):
         flux_block(block, gather_block(block, 0, bins)[1])
+        for piece in range(bins // quad_blocks // sign_part):
+            row = block * (bins // quad_blocks) + piece * sign_part
+            sign_rows(pl.multiple_of(row, sign_part), sign_part)
 
     pl.semaphore_wait(barrier, peers - 1)
     source_and_lon(0, energy / bins)
@@ -406,9 +425,7 @@
     near_track = table_pick(table, near_lane, lax.div(near_point, LANES))
     target = wave_height + OBS_GAIN * (near_hs - near_track)
     ratio = jnp.maximum(target, 0.5 * wave_height) / (wave_height + 1e-6)
-    scale = ratio * ratio
-    for start, size in chunks:
-        out_ref[pl.ds(start, size), :] = masked_ref[pl.ds(start, size), :] * scale
+    scale_ref[...] = ratio * ratio
 
     for step in range(STEPS):
         for c in range(len(chunks)):
@@ -427,6 +444,11 @@
     @pl.loop(1, peers)
     def _(offset):
         height_copy(offset, peer_id(offset)[1]).wait_send()
+
+
+def finish(masked_ref, track_in, scale_ref, out_ref, track_out):
+    out_ref[...] = masked_ref[...] * scale_ref[...]
+    track_out[...] = track_in[...]
 
 
 def body(
@@ -453,27 +475,24 @@
     wide = -(-most // LANES) * LANES
     quad_block = block_rows(quads, 432)
     peers = pts_total * sub_total
-    cols = jnp.stack([growth, damping, courant[0], courant[1], coupling], axis=1)
-    codes = lax.dynamic_slice_in_dim(upwind, lax.axis_index("pts") * LANES, LANES, 3)[:, :, 0]
-    codes = jnp.concatenate([codes, codes], axis=1)
     f32, bf16 = jnp.float32, jnp.bfloat16
     count = len(chunks)
     vmem = pl.BlockSpec(memory_space=pltpu.VMEM)
-    analysis, track = pl.pallas_call(
+    masked, track, scale = pl.pallas_call(
         functools.partial(kernel, pts_total, sub_total, chunks, quad_block),
         out_shape=(
             jax.ShapeDtypeStruct((bins, LANES), f32),
             jax.ShapeDtypeStruct((1, observations), f32),
+            jax.ShapeDtypeStruct((1, LANES), f32),
         ),
-        in_specs=[vmem] * 11,
-        out_specs=(vmem, vmem),
+        in_specs=[vmem] * 13,
+        out_specs=(vmem, vmem, vmem),
         scratch_shapes=[
             pltpu.VMEM((4 * quads, bins), bf16),
             pltpu.VMEM((bins, quads), bf16),
             pltpu.VMEM((4 * quads, LANES), f32),
             pltpu.VMEM((bins, 2 * LANES), bf16),
             pltpu.VMEM((quads, 2 * LANES), bf16),
-            pltpu.VMEM((bins, LANES), f32),
             pltpu.VMEM((bins, LANES), f32),
             pltpu.VMEM((STEPS, bins, LANES), f32),
             pltpu.VMEM((STEPS, bins, LANES), f32),
@@ -484,6 +503,10 @@
             pltpu.VMEM((STEPS, count, 2, 8, wide), f32),
             pltpu.VMEM((LANES, observations), bf16),
             pltpu.VMEM((peers, 8, LANES), f32),
+            pltpu.VMEM((bins, 8), f32),
+            pltpu.VMEM((quads, 8), jnp.int32),
+            pltpu.VMEM((2, TILE, LANES), jnp.int32),
+            pltpu.VMEM((8, -(-max(bins, quads) // LANES) * LANES), f32),
         ]
         + [pltpu.SemaphoreType.DMA((STEPS, count))] * 8
         + [pltpu.SemaphoreType.DMA((peers,))] * 2,
@@ -494,15 +517,27 @@
         spectra.reshape(bins, LANES),
         sea_mask,
         wind_speed,
-        cols,
-        quartets,
+        growth,
+        damping,
+        courant,
+        coupling,
         quartets.T,
-        codes,
+        upwind.reshape(-1, LANES),
         obs_point.reshape(1, observations),
         obs_point.reshape(-1, LANES),
         obs_hs.reshape(-1, LANES),
         nearest,
     )
+    analysis, track = pl.pallas_call(
+        finish,
+        out_shape=(
+            jax.ShapeDtypeStruct((bins, LANES), f32),
+            jax.ShapeDtypeStruct((1, observations), f32),
+        ),
+        in_specs=[vmem] * 3,
+        out_specs=(vmem, vmem),
+        compiler_params=pltpu.CompilerParams(vmem_limit_bytes=8 * 1024 * 1024),
+    )(masked, track, scale)
     return analysis.reshape(bins, 1, LANES), track.reshape(observations)
 
 

time: 79.4 us -> 68.9 us (0.87)
  Pallas kernels: 71.6 us -> 65.6 us
  local copies, waits for them, and re-layouts: 6.23 us -> 2.37 us
    pallas_call x1, Pallas kernels: 71.6 us -> 64.7 us  [body(): pl.pallas_call(functools.partial(kernel, pts_total, sub_total, chunks, qu...]
    unnamed x17 -> x6, local copies, waits for them, and re-layouts: 4.98 us -> 2.37 us
    another operation x6 -> x0, local copies, waits for them, and re-layouts: 1.19 us -> none  [body(): jnp.stack([growth, damping, courant[0], courant[1], coupling], axis=1)]
    pallas_call x0 -> x1, Pallas kernels: none -> 0.89 us  [body(): pl.pallas_call(finish, out_shape=(jax.ShapeDtypeStruct((bins, LANES), f32...]
where the time goes in v2:
time: 68.9 us; the launch traced here: 68.6 us
  Pallas kernels  65.6 us (95%)
  local copies, waits for them, and re-layouts  2.37 us (3%)
    pallas_call x1, Pallas kernels, body(): pl.pallas_call(functools.partial(kernel, pts_total, sub_total, chunks, qu...  64.7 us
    unnamed x6, local copies, waits for them, and re-layouts  2.37 us

profile of v2, /device:TPU:0, one launch (start us, length us, event | category | flops | bytes accessed | tf_op | source)
XLA Modules:
  0.0 68.6 jit_solution(5483508625018854371)
XLA Ops:
  0.6 64.7 %shard_map.131 = (f32[1296,128]{1,0:T(8,128)}, f32[1,4096]{1,0:T(1,128)}, f32[1,128]{1,0:T(1,128)}) custom-call(f32[1296,128]{1,0:T(8,128)} %bitcast.10, s32[1,128]{1,0:T(1,128)} %mask_ref.1, f32[1,128]{1,0:T(1,128)} %wind_ref.1, f32[1296]{0:T(1024)} %growth_ref.1, f32[1296]{0:T(1024)} %damping_ref.1, f32[2,1296]{1,0:T(2,128)} %courant_ref.1, ...), custom_call_target="tpu_custom_call" | custom-call | tf_op jit(solution)/shard_map/pallas_call | solution.py:481
  65.3 0.0 copy-start.2
  65.3 0.6 copy-done.2
  65.9 0.0 copy-start
  65.9 1.1 %copy-done = f32[1296,128]{1,0:T(8,128)S(1)} copy-done((f32[1296,128]{1,0:T(8,128)S(1)}, f32[1296,128]{1,0:T(8,128)}, u32[]{:S(2)}) %copy-start) | copy-done | bytes 663576
  67.0 0.0 copy-start.1
  67.0 0.7 %copy-done.1 = f32[1,4096]{1,0:T(1,128)S(1)} copy-done((f32[1,4096]{1,0:T(1,128)S(1)}, f32[1,4096]{1,0:T(1,128)}, u32[]{:S(2)}) %copy-start.1) | copy-done | bytes 16408
  67.7 0.9 %shard_map.132 = (f32[1296,128]{1,0:T(8,128)}, f32[1,4096]{1,0:T(1,128)}) custom-call(f32[1296,128]{1,0:T(8,128)S(1)} %copy-done, f32[1,4096]{1,0:T(1,128)S(1)} %copy-done.1, f32[1,128]{1,0:T(1,128)S(1)} %copy-done.2), custom_call_target="tpu_custom_call" | custom-call | tf_op jit(solution)/shard_map/pallas_call | solution.py:531
Async XLA Ops:
  65.3 0.6 copy-start.2
  65.9 1.1 %copy-start = (f32[1296,128]{1,0:T(8,128)S(1)}, f32[1296,128]{1,0:T(8,128)}, u32[]{:S(2)}) copy-start(f32[1296,128]{1,0:T(8,128)} %get-tuple-element.7.masked_ref) | copy-start | bytes 1990660
  67.0 0.7 %copy-start.1 = (f32[1,4096]{1,0:T(1,128)S(1)}, f32[1,4096]{1,0:T(1,128)}, u32[]{:S(2)}) copy-start(f32[1,4096]{1,0:T(1,128)} %get-tuple-element.8.track_in) | copy-start | bytes 49156

commit v3 on v2

--- a/solution.py
+++ b/solution.py
@@ -166,16 +166,17 @@
     one16 = jnp.bfloat16(1)
     zero16 = jnp.bfloat16(0)
 
-    @pl.loop(0, quad_blocks)
-    def _(block):
-        for member_of_quad in range(4):
-            row = pl.multiple_of(block * quad_block, quad_block)
-            index = quad_ref[pl.ds(row, quad_block), member_of_quad : member_of_quad + 1]
-            lanes = lax.broadcasted_iota(jnp.int32, (quad_block, bins), 1).astype(jnp.int16)
-            index = jnp.broadcast_to(index, (quad_block, LANES)).astype(jnp.int16)
-            index = jnp.concatenate([index] * (-(-bins // LANES)), axis=1)[:, :bins]
-            to = pl.multiple_of(block * (4 * quad_block) + member_of_quad * quad_block, quad_block)
-            picks[pl.ds(to, quad_block), :] = jnp.where(lanes == index, one16, zero16)
+    def pick_rows(block, member_of_quad):
+        row = pl.multiple_of(block * quad_block, quad_block)
+        index = quad_ref[pl.ds(row, quad_block), member_of_quad : member_of_quad + 1]
+        lanes = lax.broadcasted_iota(jnp.int32, (quad_block, bins), 1).astype(jnp.int16)
+        index = jnp.broadcast_to(index, (quad_block, LANES)).astype(jnp.int16)
+        index = jnp.concatenate([index] * (-(-bins // LANES)), axis=1)[:, :bins]
+        to = pl.multiple_of(block * (4 * quad_block) + member_of_quad * quad_block, quad_block)
+        hot = jnp.where(lanes == index, one16, zero16)
+        picks[pl.ds(to, quad_block), :] = hot
+        got = jnp.dot(hot, split_values[...], preferred_element_type=jnp.float32)
+        return got[:, :LANES] + got[:, LANES:]
 
     def sign_rows(row, size):
         rows = (lax.broadcasted_iota(jnp.int32, (size, quads), 0) + row).astype(jnp.int16)
@@ -350,7 +351,7 @@
 
     @pl.loop(0, quad_blocks)
     def _(block):
-        flux_block(block, gather_block(block, 0, bins)[1])
+        flux_block(block, jnp.concatenate([pick_rows(block, k) for k in range(4)], axis=0))
         for piece in range(bins // quad_blocks // sign_part):
             row = block * (bins // quad_blocks) + piece * sign_part
             sign_rows(pl.multiple_of(row, sign_part), sign_part)
@@ -536,7 +537,7 @@
         ),
         in_specs=[vmem] * 3,
         out_specs=(vmem, vmem),
-        compiler_params=pltpu.CompilerParams(vmem_limit_bytes=8 * 1024 * 1024),
+        compiler_params=pltpu.CompilerParams(vmem_limit_bytes=56 * 1024 * 1024),
     )(masked, track, scale)
     return analysis.reshape(bins, 1, LANES), track.reshape(observations)
 

time: 68.9 us -> 66.6 us (0.967)
  local copies, waits for them, and re-layouts: 2.37 us -> 0 us
    unnamed x6 -> x0, local copies, waits for them, and re-layouts: 2.37 us -> none
    pallas_call x1, Pallas kernels: 0.89 us -> 2 us  [body(): pl.pallas_call(finish, out_shape=(jax.ShapeDtypeStruct((bins, LANES), f32...]
    pallas_call x1, Pallas kernels: 64.7 us -> 63.8 us  [body(): pl.pallas_call(functools.partial(kernel, pts_total, sub_total, chunks, qu...]
where the time goes in v3:
time: 66.6 us; the launch traced here: 66.5 us
  Pallas kernels  65.8 us (99%)
    pallas_call x1, Pallas kernels, body(): pl.pallas_call(functools.partial(kernel, pts_total, sub_total, chunks, qu...  63.8 us
    pallas_call x1, Pallas kernels, body(): pl.pallas_call(finish, out_shape=(jax.ShapeDtypeStruct((bins, LANES), f32...  2 us

profile of v3, /device:TPU:0, one launch (start us, length us, event | category | flops | bytes accessed | tf_op | source)
XLA Modules:
  0.0 66.5 jit_solution(9684722200380059227)
XLA Ops:
  0.6 63.8 %shard_map.131 = (f32[1296,128]{1,0:T(8,128)}, f32[1,4096]{1,0:T(1,128)}, f32[1,128]{1,0:T(1,128)}) custom-call(f32[1296,128]{1,0:T(8,128)} %bitcast.10, s32[1,128]{1,0:T(1,128)} %mask_ref.1, f32[1,128]{1,0:T(1,128)} %wind_ref.1, f32[1296]{0:T(1024)} %growth_ref.1, f32[1296]{0:T(1024)} %damping_ref.1, f32[2,1296]{1,0:T(2,128)} %courant_ref.1, ...), custom_call_target="tpu_custom_call" | custom-call | tf_op jit(solution)/shard_map/pallas_call | solution.py:482
  64.5 2.0 %shard_map.132 = (f32[1296,128]{1,0:T(8,128)}, f32[1,4096]{1,0:T(1,128)}) custom-call(f32[1296,128]{1,0:T(8,128)} %get-tuple-element.7.masked_ref, f32[1,4096]{1,0:T(1,128)} %get-tuple-element.8.track_in, f32[1,128]{1,0:T(1,128)} %get-tuple-element.9.scale_ref), custom_call_target="tpu_custom_call" | custom-call | tf_op jit(solution)/shard_map/pallas_call | solution.py:532
